TPU v7x, 128 devices: a whole 4x4x4 slice. The times are simulated.
128 devices in a mesh: dp: 32 (over y, x_lo, z), mp: 4 (over x_hi, core).
Axes of the slice: x: 4 (x_hi: 2, x_lo: 2; x = x_hi * 2 + x_lo), y: 4, z: 4, core: 2. Of those that a mesh axis runs over, the one named last changes fastest.
Arguments:
- tokens: bfloat16 [96, 256, 1024], P('dp', 'mp'), may hold values from -6 to 6
- clear_count: int32 [96, 256], P('dp', 'mp'), may hold values from 0 to 256
- gain_one: float32 [1024], replicated, may hold values from 0.25 to 1.75
- spatial_qkv: bfloat16 [3, 1024, 1024], P(None, None, 'mp'), as said below
- spatial_out: bfloat16 [1024, 1024], P('mp'), may hold values from -0.1875 to 0.1875
- gain_two: float32 [1024], replicated, may hold values from 0.25 to 1.75
- mlp_up: bfloat16 [1024, 4096], P(None, 'mp'), may hold values from -0.1875 to 0.1875
- mlp_down: bfloat16 [4096, 1024], P('mp'), may hold values from -0.09375 to 0.09375
- gain_three: float32 [1024], replicated, may hold values from 0.25 to 1.75
- temporal_qkv: bfloat16 [3, 1024, 1024], replicated, as said below
- temporal_out: bfloat16 [1024, 1024], replicated, may hold values from -0.1875 to 0.1875
Outputs:
- joined: bfloat16 [96, 4, 64, 1024], P(None, 'mp', 'dp')
Inputs may be any that keep to these rules, and one draw needn't show every extreme that they name: `spatial_qkv`: each of the three 1024 x 1024 matrices has entries of order 1024^-0.5 times a factor of at most 40; nothing else is promised. `temporal_qkv`: as for spatial_qkv.
All inputs are finite; a program needn't handle non-finite values.
Results may differ from a plain program's by a relative error of at most 0.02.
Values may be sent and summed in bfloat16 or wider, within the bound.
A program may use at most 64 MiB of HBM per device.

v0:
```python
import math

import jax
import jax.numpy as jnp
from jax import lax
from jax.sharding import PartitionSpec as P

HEADS = 16
HD = 64
PIX = 256
FRAMES = 12


EPS = 1e-06


def normalize(rows, gain):
    mean = jnp.mean(rows, axis=-1, keepdims=True)
    centered = rows - mean
    spread = jnp.mean(centered * centered, axis=-1, keepdims=True)
    return centered * lax.rsqrt(spread + EPS) * gain


def softmax_rows(scores):
    top = jnp.max(scores, axis=-1, keepdims=True)
    expo = jnp.exp(scores - top)
    return expo / jnp.sum(expo, axis=-1, keepdims=True)


def temporal_block(spatial, projected, counts, temporal_out):
    seqs, single, items, width = spatial.shape
    tiles = seqs // FRAMES
    scale = 1.0 / math.sqrt(HD)
    parts = projected.reshape(tiles, FRAMES, items, 3, HEADS, HD)
    bias = jnp.log((counts.astype(jnp.float32) + 1.0) / (PIX + 1.0)).reshape(tiles, FRAMES, items)
    bias = jnp.transpose(bias, (0, 2, 1))[:, :, None, None, :]
    scores = (
        jnp.einsum(
            "tfphe,tgphe->tphfg",
            parts[:, :, :, 0],
            parts[:, :, :, 1],
            preferred_element_type=jnp.float32,
        )
        * scale
        + bias
    )
    probs = softmax_rows(scores).astype(jnp.bfloat16)
    mixed = jnp.einsum(
        "tphfg,tgphe->tfphe", probs, parts[:, :, :, 2], preferred_element_type=jnp.float32
    ).astype(jnp.bfloat16)
    mixed = mixed.reshape(seqs, single, items, width)
    update = jnp.einsum("sipc,cd->sipd", mixed, temporal_out, preferred_element_type=jnp.float32)
    return (spatial.astype(jnp.float32) + update).astype(jnp.bfloat16)


def temporal_project(spatial, gain_three, temporal_qkv):
    normed = normalize(spatial.astype(jnp.float32), gain_three).astype(jnp.bfloat16)
    projected = jnp.einsum(
        "...d,idc->...ic", normed, temporal_qkv, preferred_element_type=jnp.float32
    ).astype(jnp.bfloat16)
    return projected.reshape(spatial.shape[:-1] + (3 * spatial.shape[-1],))


def local(
    tokens,
    clear_count,
    gain_one,
    spatial_qkv,
    spatial_out,
    gain_two,
    mlp_up,
    mlp_down,
    gain_three,
    temporal_qkv,
    temporal_out,
):
    frames, part_rows, width = tokens.shape
    local_cols = spatial_qkv.shape[2]
    local_heads = local_cols // HD
    scale = 1.0 / math.sqrt(HD)
    mp_index = lax.axis_index("mp")
    piece = lax.all_gather(tokens, "mp", axis=1, tiled=True)
    normed = normalize(piece.astype(jnp.float32), gain_one).astype(jnp.bfloat16)
    qkv = jnp.einsum(
        "spd,idc->spic", normed, spatial_qkv, preferred_element_type=jnp.float32
    ).astype(jnp.bfloat16)
    qkv, whole_tokens = (qkv, piece)
    patches = qkv.shape[1]
    query = qkv[:, :, 0].reshape(frames, patches, local_heads, HD)
    key_all = qkv[:, :, 1].reshape(frames, patches, local_heads, HD)
    value = qkv[:, :, 2].reshape(frames, patches, local_heads, HD)
    scores = (
        jnp.einsum("sqhe,skhe->shqk", query, key_all, preferred_element_type=jnp.float32) * scale
    )
    probs = softmax_rows(scores).astype(jnp.bfloat16)
    mixed = jnp.einsum("shqk,skhe->sqhe", probs, value, preferred_element_type=jnp.float32).astype(
        jnp.bfloat16
    )
    mixed = mixed.reshape(frames, patches, local_cols)
    term = jnp.einsum("spc,cd->spd", mixed, spatial_out, preferred_element_type=jnp.float32)
    full_resid = whole_tokens.astype(jnp.float32) + lax.psum(
        term.astype(jnp.bfloat16), "mp"
    ).astype(jnp.float32)
    hidden = jax.nn.gelu(
        jnp.einsum(
            "spd,df->spf",
            normalize(full_resid, gain_two).astype(jnp.bfloat16),
            mlp_up,
            preferred_element_type=jnp.float32,
        ),
        approximate=False,
    ).astype(jnp.bfloat16)
    partial_sum = jnp.einsum("spf,fd->spd", hidden, mlp_down, preferred_element_type=jnp.float32)
    resid = lax.dynamic_slice_in_dim(full_resid, mp_index * part_rows, part_rows, 1)
    spatial = (
        resid
        + lax.psum_scatter(
            partial_sum.astype(jnp.bfloat16), "mp", scatter_dimension=1, tiled=True
        ).astype(jnp.float32)
    ).astype(jnp.bfloat16)
    dp_count = lax.axis_size("dp")
    pair = part_rows // dp_count
    parcel = spatial.reshape(frames, dp_count, pair, width)
    counts_local = clear_count.astype(jnp.bfloat16).reshape(frames, dp_count, pair)
    arrived = lax.all_to_all(parcel, "dp", split_axis=1, concat_axis=0, tiled=True)
    arrived_counts = lax.all_to_all(counts_local, "dp", split_axis=1, concat_axis=0, tiled=True)
    projected = temporal_project(arrived, gain_three, temporal_qkv)
    return temporal_block(arrived, projected, arrived_counts, temporal_out)


def solution(mesh):
    placed = (
        P("dp", "mp", None),
        P("dp", "mp"),
        P(),
        P(None, None, "mp"),
        P("mp", None),
        P(),
        P(None, "mp"),
        P("mp", None),
        P(),
        P(),
        P(),
    )
    return jax.shard_map(
        local, mesh=mesh, in_specs=placed, out_specs=P(None, "mp", "dp", None), check_vma=False
    )
```

profile of v0, /device:TPU:1, one launch (start us, length us, event | category | flops | bytes accessed | tf_op | source)
XLA Modules:
  0.0 203.6 jit_solution(16438198415523960203)
XLA Ops:
  7.3 29.0 %all-gather.2.cloned.1.call-done = bf16[3,256,1024]{2,1,0:T(8,128)(2,1)} async-done(((bf16[3,64,1024]{2,1,0:T(8,128)(2,1)}), bf16[3,256,1024]{2,1,0:T(8,128)(2,1)}) %all-gather.2.cloned.1.call-update) | async-done | bytes 1572880 | tf_op jit(solution)/shard_map/all_gather | solution.py:82
  36.4 1.8 convert_reduce_fusion
  38.2 2.0 fusion.6
  40.2 1.9 fusion.74
  42.2 2.9 %fusion.144 = (f32[3,4,256]{2,1,0:T(4,128)S(1)}, f32[3,4,256,256]{2,3,1,0:T(8,128)}) fusion(bf16[3,256,4,64]{1,3,2,0:T(8,128)(2,1)S(1)} %bitcast.121, bf16[3,256,4,64]{1,3,2,0:T(8,128)(2,1)S(1)} %bitcast.120), kind=kOutput, calls=%fused_computation.166 | convolution fusion | flops 103022848 | bytes 3944448 | tf_op jit(solution)/shard_map/sub | solution.py:26
  45.0 2.3 %fusion.89 = bf16[3,4,64,256]{3,2,1,0:T(8,128)(2,1)S(1)} fusion(bf16[3,256,4,64]{1,3,2,0:T(8,128)(2,1)S(1)} %bitcast.119, f32[3,4,256,256]{2,3,1,0:T(8,128)} %get-tuple-element.16, f32[3,4,256]{2,1,0:T(4,128)S(1)} %get-tuple-element.15), kind=kOutput, calls=%fused_computation.99 | convolution fusion | flops 102432768 | bytes 3944448 | tf_op jit(solution)/shard_map/shqk,skhe->sqhe/dot_general | solution.py:96
  47.4 1.8 convolution_convert_fusion
  49.2 50.6 %all-reduce.2.cloned.1.call-done = bf16[3,256,1024]{2,1,0:T(8,128)(2,1)} async-done(((bf16[3,256,1024]{2,1,0:T(8,128)(2,1)}), bf16[3,256,1024]{2,1,0:T(8,128)(2,1)}) %all-reduce.2.cloned.1.call-update) | async-done | bytes 1572880 | tf_op jit(solution)/shard_map/psum | solution.py:101
  99.9 4.1 %convert_add_fusion = (f32[3,256,1024]{2,1,0:T(8,128)}, f32[3,256]{1,0:T(4,128)S(1)}) fusion(bf16[3,256,1024]{2,1,0:T(8,128)(2,1)} %all-gather.2.cloned.1.call-done, bf16[3,256,1024]{2,1,0:T(8,128)(2,1)} %all-reduce.2.cloned.1.call-done), kind=kLoop, calls=%fused_computation.5 | loop fusion | flops 3144960 | bytes 6294528 | tf_op jit(solution)/shard_map/add | solution.py:101
  104.7 2.6 %fusion.100 = (u8[256,1024]{1,0:T(8,128)(4,1)S(1)}, u8[256,1024]{1,0:T(8,128)(4,1)S(1)}, f32[3,256,1024]{2,1,0:T(8,128)S(1)}) fusion(bf16[1024,1024]{1,0:T(8,128)(2,1)S(1)} %copy-done, f32[1024]{0:T(1024)S(1)} %copy-done.10, f32[3,256]{1,0:T(4,128)S(1)} %add_rsqrt_fusion.1, f32[3,256]{1,0:T(4,128)S(1)} %broadcast_multiply_fusion.1, ...), kind=kOutput, calls=%fused_computation.115 | convolution fusion | flops 1625817088 | bytes 8923136 | tf_op jit(solution)/shard_map/spd,df->spf/dot_general | solution.py:105
  107.4 9.7 %fusion.28 = bf16[3,256,1024]{2,1,0:T(8,128)(2,1)} fusion(bf16[1024,1024]{1,0:T(8,128)(2,1)S(1)} %copy-done.7, f32[3,256,1024]{2,1,0:T(8,128)S(1)} %get-tuple-element.17, u8[256,1024]{1,0:T(8,128)(4,1)S(1)} %get-tuple-element.6, u8[256,1024]{1,0:T(8,128)(4,1)S(1)} %get-tuple-element.5), kind=kOutput, calls=%fused_computation.50 | convolution fusion | flops 1666449408 | bytes 7340032 | tf_op jit(solution)/shard_map/spf,fd->spd/dot_general | solution.py:113
  117.8 7.0 %all-to-all-start.1 = ((bf16[3,32,2]{0,2,1:T(2,128)(2,1)}), bf16[3,32,2]{0,2,1:T(2,128)(2,1)S(1)}, u32[]{:S(2)}, u32[]{:S(2)}) async-start(bf16[3,32,2]{0,2,1:T(2,128)(2,1)} %bitcast.21), calls=%async_computation.2 | async-start | bytes 32768 | tf_op jit(solution)/shard_map/all_to_all | solution.py:126
  124.8 26.7 %reduce-scatter.2.cloned.1.call-done = bf16[3,64,1024]{2,1,0:T(8,128)(2,1)} async-done(((bf16[3,256,1024]{2,1,0:T(8,128)(2,1)}), bf16[3,64,1024]{2,1,0:T(8,128)(2,1)}) %reduce-scatter.2.cloned.1.call-update) | async-done | bytes 393232 | tf_op jit(solution)/shard_map/reduce_scatter | solution.py:117
  151.4 1.3 add_convert_fusion
  154.0 7.0 %all-to-all-start = ((bf16[3,32,2,1024]{3,2,0,1:T(2,128)(2,1)}), bf16[3,32,2,1024]{3,2,0,1:T(2,128)(2,1)S(1)}, u32[]{:S(2)}, u32[]{:S(2)}) async-start(bf16[3,32,2,1024]{3,2,0,1:T(2,128)(2,1)} %copy.62), calls=%async_computation.1 | async-start | bytes 786432 | tf_op jit(solution)/shard_map/all_to_all | solution.py:125
  161.3 8.4 %all-to-all-done = bf16[3,32,2,1024]{3,2,0,1:T(2,128)(2,1)S(1)} async-done(((bf16[3,32,2,1024]{3,2,0,1:T(2,128)(2,1)}), bf16[3,32,2,1024]{3,2,0,1:T(2,128)(2,1)S(1)}, u32[]{:S(2)}, u32[]{:S(2)}) %all-to-all-start) | async-done | bytes 393248 | tf_op jit(solution)/shard_map/all_to_all | solution.py:125
  171.7 5.2 %fusion.79 = bf16[96,2,3,1024]{3,0,2,1:T(8,128)(2,1)} fusion(bf16[3,1024,1024]{2,1,0:T(8,128)(2,1)} %param.20, bf16[96,2,1024,1]{2,1,0,3:T(2,128)(2,1)S(1)} %fusion.105), kind=kOutput, calls=%fused_computation.94 | convolution fusion | flops 1208549376 | bytes 7864320 | tf_op jit(solution)/shard_map/...d,idc->...ic/dot_general | solution.py:58
  176.9 4.2 %reshape_reshape.3 = bf16[8,12,2,3,16,64]{5,4,1,0,3,2:T(8,128)(2,1)} reshape(bf16[96,2,3,1024]{3,0,2,1:T(8,128)(2,1)} %fusion.79) | data formatting | bytes 2359296 | tf_op jit(solution)/shard_map/reshape;reshape | solution.py:34
  181.1 3.2 %fusion.142 = (bf16[8,12,2,1,16,64]{5,4,1,0,3,2:T(8,128)(2,1)}, bf16[8,12,2,1,16,64]{5,4,1,0,3,2:T(8,128)(2,1)}, bf16[8,12,2,1,16,64]{5,4,1,0,3,2:T(8,128)(2,1)}) fusion(bf16[8,12,2,3,16,64]{5,4,1,0,3,2:T(8,128)(2,1)} %reshape_reshape.3), kind=kLoop, calls=%fused_computation.164 | loop fusion | bytes 2359296 | tf_op jit(solution)/shard_map/slice | solution.py:49
  184.2 4.1 %fusion.145 = (f32[8,2,16,12]{3,2,1,0:T(8,128)S(1)}, f32[8,2,16,12,12]{3,4,2,1,0:T(8,128)}) fusion(f32[8,2,12]{2,1,0:T(2,128)S(1)} %copy.77, bf16[8,12,2,1,16,64]{5,4,1,0,3,2:T(8,128)(2,1)} %get-tuple-element.11, bf16[8,12,2,1,16,64]{5,4,1,0,3,2:T(8,128)(2,1)} %get-tuple-element.10), kind=kOutput, calls=%fused_computation.167 | convolution fusion | flops 4866059 | bytes 946944 | tf_op jit(solution)/shard_map/sub | solution.py:26
  188.3 2.4 %fusion.82 = bf16[8,12,2,16,64]{4,1,3,2,0:T(8,128)(2,1)S(1)} fusion(f32[8,2,16,12,12]{3,4,2,1,0:T(8,128)} %get-tuple-element.19, bf16[8,12,2,1,16,64]{5,4,1,0,3,2:T(8,128)(2,1)} %get-tuple-element.9, f32[8,2,16,12]{3,2,1,0:T(8,128)S(1)} %get-tuple-element.18), kind=kOutput, calls=%fused_computation.96 | convolution fusion | flops 4988928 | bytes 946176 | tf_op jit(solution)/shard_map/tphfg,tgphe->tfphe/dot_general | solution.py:48
  191.8 1.8 reshape.131
  193.6 2.3 %fusion.90 = bf16[96,1,2,1024]{3,0,2,1:T(8,128)(2,1)S(1)} fusion(bf16[96,2,1024]{2,0,1:T(8,128)(2,1)S(1)} %reshape.131, bf16[1024,1024]{1,0:T(8,128)(2,1)} %param.21, f32[96,2,1024]{2,1,0:T(2,128)S(1)} %bitcast.118), kind=kOutput, calls=%fused_computation.100 | convolution fusion | flops 403046400 | bytes 3670016 | tf_op jit(solution)/shard_map/sipc,cd->sipd/dot_general | solution.py:52
  195.9 1.2 copy.81
  (53 shorter events, 6.9 us)
Async XLA Ops:
  6.5 98.2 %copy-start = (bf16[1024,1024]{1,0:T(8,128)(2,1)S(1)}, bf16[1024,1024]{1,0:T(8,128)(2,1)}, u32[]{:S(2)}) copy-start(bf16[1024,1024]{1,0:T(8,128)(2,1)} %param.17) | copy-start | bytes 6291460
  6.5 33.7 %copy-start.9 = (f32[1024]{0:T(1024)S(1)}, f32[1024]{0:T(1024)}, u32[]{:S(2)}) copy-start(f32[1024]{0:T(1024)} %param.13) | copy-start | bytes 12292
  6.5 29.8 %all-gather.2.cloned.1.call-start = ((), (), s32[]{:S(2)}) async-start(), calls=%async_computation.3 | async-start | bytes 1966080 | tf_op jit(solution)/shard_map/all_gather | solution.py:82
  7.3 92.6 %all-reduce.2.cloned.1.call-start = ((), (), s32[]{:S(2)}) async-start(), calls=%async_computation.4 | async-start | bytes 3145728 | tf_op jit(solution)/shard_map/psum | solution.py:101
  36.4 3.8 %copy-start.1 = (bf16[3,256,1024]{2,1,0:T(8,128)(2,1)S(1)}, bf16[3,256,1024]{2,1,0:T(8,128)(2,1)}, u32[]{:S(2)}) copy-start(bf16[3,256,1024]{2,1,0:T(8,128)(2,1)} %all-gather.2.cloned.1.call-done) | copy-start | bytes 4718596
  36.4 3.9 %copy-start.8 = (bf16[3,1024,256]{2,1,0:T(8,128)(2,1)S(1)}, bf16[3,1024,256]{2,1,0:T(8,128)(2,1)}, u32[]{:S(2)}) copy-start(bf16[3,1024,256]{2,1,0:T(8,128)(2,1)} %param.14) | copy-start | bytes 4718596
  45.0 2.4 %copy-start.4 = (bf16[256,1024]{1,0:T(8,128)(2,1)S(1)}, bf16[256,1024]{1,0:T(8,128)(2,1)}, u32[]{:S(2)}) copy-start(bf16[256,1024]{1,0:T(8,128)(2,1)} %param.15) | copy-start | bytes 1572868
  49.2 102.3 %reduce-scatter.2.cloned.1.call-start = ((), (), s32[]{:S(2)}) async-start(), calls=%async_computation.5 | async-start | bytes 1966080 | tf_op jit(solution)/shard_map/reduce_scatter | solution.py:117
  99.9 4.1 %copy-start.2 = (bf16[3,256,1024]{2,1,0:T(8,128)(2,1)S(1)}, bf16[3,256,1024]{2,1,0:T(8,128)(2,1)}, u32[]{:S(2)}) copy-start(bf16[3,256,1024]{2,1,0:T(8,128)(2,1)} %all-gather.2.cloned.1.call-done) | copy-start | bytes 4718596
  99.9 4.1 %copy-start.3 = (bf16[3,256,1024]{2,1,0:T(8,128)(2,1)S(1)}, bf16[3,256,1024]{2,1,0:T(8,128)(2,1)}, u32[]{:S(2)}) copy-start(bf16[3,256,1024]{2,1,0:T(8,128)(2,1)} %all-reduce.2.cloned.1.call-done) | copy-start | bytes 4718596
  104.0 0.7 copy-start.10
  104.7 2.6 %copy-start.7 = (bf16[1024,1024]{1,0:T(8,128)(2,1)S(1)}, bf16[1024,1024]{1,0:T(8,128)(2,1)}, u32[]{:S(2)}) copy-start(bf16[1024,1024]{1,0:T(8,128)(2,1)} %param.18) | copy-start | bytes 6291460
  107.3 9.7 %copy-start.6 = (s32[3,64]{1,0:T(4,128)S(1)}, s32[3,64]{1,0:T(4,128)}, u32[]{:S(2)}) copy-start(s32[3,64]{1,0:T(4,128)} %param.12) | copy-start | bytes 2308
  117.8 36.2 %all-to-all-start.1 = ((bf16[3,32,2]{0,2,1:T(2,128)(2,1)}), bf16[3,32,2]{0,2,1:T(2,128)(2,1)S(1)}, u32[]{:S(2)}, u32[]{:S(2)}) async-start(bf16[3,32,2]{0,2,1:T(2,128)(2,1)} %bitcast.21), calls=%async_computation.2 | async-start | bytes 32768 | tf_op jit(solution)/shard_map/all_to_all | solution.py:126
  151.4 19.7 %copy-start.5 = (f32[1024]{0:T(1024)S(1)}, f32[1024]{0:T(1024)}, u32[]{:S(2)}) copy-start(f32[1024]{0:T(1024)} %param.19) | copy-start | bytes 12292
  154.0 15.6 %all-to-all-start = ((bf16[3,32,2,1024]{3,2,0,1:T(2,128)(2,1)}), bf16[3,32,2,1024]{3,2,0,1:T(2,128)(2,1)S(1)}, u32[]{:S(2)}, u32[]{:S(2)}) async-start(bf16[3,32,2,1024]{3,2,0,1:T(2,128)(2,1)} %copy.62), calls=%async_computation.1 | async-start | bytes 786432 | tf_op jit(solution)/shard_map/all_to_all | solution.py:125
Sparse Core Ops, SparseCore 0:
  9.0 27.2 all-gather.1
  49.3 50.5 all-reduce.1
  117.2 34.2 reduce-scatter.1
where the time goes:
time: 205 us; the launch traced here: 204 us
  waiting for transfers between devices  115 us (56%)
  matrix products  35.1 us (17%)
  starting transfers between devices  14 us (7%)
  local copies, waits for them, and re-layouts  13.7 us (7%)
  between operations  13.4 us (7%)
  other arithmetic  12 us (6%)
    psum x1, waiting for transfers between devices, local(): lax.psum(term.astype(jnp.bfloat16), 'mp').astype(jnp.float32)  50.6 us
    all_gather x1, waiting for transfers between devices, local(): piece = lax.all_gather(tokens, 'mp', axis=1, tiled=True)  29 us
    reduce_scatter x1, waiting for transfers between devices, local(): lax.psum_scatter(partial_sum.astype(jnp.bfloat16), 'mp', scatter_dimensio...  26.7 us
    dot_general x1, matrix products, local(): jnp.einsum('spf,fd->spd', hidden, mlp_down, preferred_element_type=jnp.fl...  9.68 us
    all_to_all x1, waiting for transfers between devices, local(): lax.all_to_all(parcel, 'dp', split_axis=1, concat_axis=0, tiled=True)  8.37 us
    all_to_all x1, starting transfers between devices, local(): lax.all_to_all(counts_local, 'dp', split_axis=1, concat_axis=0, tiled=True)  6.99 us
    all_to_all x1, starting transfers between devices, local(): lax.all_to_all(parcel, 'dp', split_axis=1, concat_axis=0, tiled=True)  6.97 us
    sub x2, matrix products, softmax_rows(): expo = jnp.exp(scores - top)  6.93 us
  transfers between devices with their start and end apart: 5, of which 4 were waited for; matrix products, arithmetic and copies ran while one was open for 2% of the time, Pallas kernels for 0%

commit v1 on v0

v1 whole, which is shorter than its diff:
```python
import math

import jax
import jax.numpy as jnp
from jax import lax
from jax.experimental import pallas as pl
from jax.experimental.pallas import tpu as pltpu
from jax.sharding import PartitionSpec as P

HD = 64
PIX = 256
FRAMES = 12
EPS = 1e-06
F = 3
N = 256
B = 64
D = 1024
C = 256
S = 96
DP = 32
BF = jnp.bfloat16
F32 = jnp.float32


def normalize(rows, gain):
    mean = jnp.sum(rows, axis=-1, keepdims=True) * (1.0 / D)
    centered = rows - mean
    spread = jnp.sum(centered * centered, axis=-1, keepdims=True) * (1.0 / D)
    return centered * lax.rsqrt(spread + EPS) * gain


def gelu(x):
    return 0.5 * x * (1.0 + lax.erf(x * (1.0 / math.sqrt(2.0))))


def at(start, size):
    return pl.ds(pl.multiple_of(start, size), size)


def dot(a, b):
    return jnp.dot(a, b, preferred_element_type=F32)


def dot_t(a, b):
    return lax.dot_general(a, b, (((1,), (1,)), ((), ())), preferred_element_type=F32)


def head_masks():
    lane = lax.broadcasted_iota(jnp.int32, (1, C), 1)
    return [(lane // HD == h) for h in range(C // HD)]


def kernel(
    tokens,
    counts,
    gain_one,
    gain_two,
    gain_three,
    w_qkv,
    w_out,
    w_up,
    w_down,
    t_qkv,
    t_out,
    out,
    tok,
    mix,
    qkv_v,
    out_v,
    up_v,
    down_v,
    tqkv_v,
    tout_v,
    normed,
    hidden,
    res,
    part,
    own,
    rs_send,
    rs_recv,
    rx_send,
    rx_recv,
    cells,
    a_send,
    a_recv,
    c_send,
    c_recv,
    tcells,
    xs,
    n3,
    q2,
    m2,
    loc,
    tok_s,
    tok_r,
    mix_s,
    mix_r,
    rs_s,
    rs_r,
    a_s,
    a_r,
    w_s,
    w_r,
):
    dp = lax.axis_index("dp")
    mp = lax.axis_index("mp")
    core = mp % 2
    sib_i = mp + 1 - 2 * core
    opp_i = (mp + 2) % 4
    diag_i = (sib_i + 2) % 4
    sib = {"mp": sib_i}
    opp = {"mp": opp_i}
    cell = (dp // 8) * 4 + dp % 4
    x_lo = (dp // 4) % 2

    def remote(src, dst, ss, rs, where):
        return pltpu.make_async_remote_copy(
            src_ref=src, dst_ref=dst, send_sem=ss, recv_sem=rs, device_id=where
        )

    def local_copy(src, dst, i):
        return pltpu.make_async_copy(src, dst, loc.at[i])

    loads = [
        local_copy(tokens, tok.at[:, at(mp * B, B)], 0),
        local_copy(w_qkv, qkv_v, 1),
        local_copy(w_out, out_v.at[at(mp * C, C)], 2),
        local_copy(w_up, up_v, 3),
        local_copy(w_down, down_v, 4),
        local_copy(t_qkv, tqkv_v, 5),
        local_copy(t_out, tout_v, 6),
    ]
    loads[0].start()
    loads[1].start()

    barrier = pltpu.get_barrier_semaphore()
    for i in range(1, 4):
        pl.semaphore_signal(barrier, inc=1, device_id={"mp": (mp + i) % 4})

    @pl.loop(1, DP)
    def _(i):
        pl.semaphore_signal(barrier, inc=1, device_id={"dp": (dp + i) % DP})

    row = lax.broadcasted_iota(jnp.int32, (8, 128), 0)
    lane = lax.broadcasted_iota(jnp.int32, (8, 128), 1)

    @pl.loop(0, DP)
    def _(d):
        tile = jnp.zeros((8, 128), jnp.int32)
        for f in range(F):
            for p in range(2):
                spot = (row == p) & (lane == dp * F + f)
                tile = jnp.where(spot, counts[f, d * 2 + p], tile)
        c_send[d] = tile.astype(F32)

    pl.semaphore_wait(barrier, DP + 2)

    first = remote(
        w_out.at[at(cell * 16, 16)],
        out_v.at[at(mp * C + cell * 16, 16)],
        w_s.at[0],
        w_r.at[0],
        opp,
    )
    first.start()

    def tok_copy(f, kind):
        blk = at(mp * B, B) if kind < 2 else at(opp_i * B, B)
        src = tokens.at[f] if kind < 2 else tok.at[f, blk]
        return remote(
            src, tok.at[f, blk], tok_s.at[kind, f], tok_r.at[kind, f], opp if kind == 0 else sib
        )

    for f in range(F):
        tok_copy(f, 0).start()
    for f in range(F):
        tok_copy(f, 1).start()
    own_w = remote(w_out, out_v.at[at(mp * C, C)], w_s.at[1], w_r.at[1], sib)
    own_w.start()
    for c in loads[2:]:
        c.start()

    c_send_own = c_send[dp]
    c_recv[dp] = c_send_own

    @pl.loop(1, DP)
    def _(i):
        to = (dp + i) % DP
        remote(c_send.at[to], c_recv.at[dp], a_s.at[F], a_r.at[F], {"dp": to}).start()

    first.wait_recv()
    mine = at(opp_i * C + cell * 16, 16)

    @pl.loop(1, 16)
    def _(j):
        q = (cell + j) % 16
        to = ((q // 4) * 2 + x_lo) * 4 + q % 4
        remote(out_v.at[mine], out_v.at[mine], w_s.at[2], w_r.at[2], {"dp": to}).start()

    masks = head_masks()

    def mix_copy(f, kind):
        cols = at(mp * C, C) if kind < 2 else at(opp_i * C, C)
        blk = mix.at[f, :, cols]
        return remote(
            blk, blk, mix_s.at[kind, f], mix_r.at[kind, f], opp if kind == 0 else sib
        )

    loads[0].wait()
    loads[1].wait()

    @pl.loop(0, F)
    def _(f):
        tok_copy(f, 0).wait_recv()
        tok_copy(f, 2).start()
        tok_copy(f, 1).wait_recv()
        tok_copy(f, 2).wait_recv()

        @pl.loop(0, N // 32)
        def _(i):
            rows = at(i * 32, 32)
            normed[rows] = normalize(tok[f, rows].astype(F32), gain_one[...]).astype(BF)

        q = dot(normed[...], qkv_v[0]) * (1.0 / math.sqrt(HD))
        k = dot(normed[...], qkv_v[1]).astype(BF)
        v = dot(normed[...], qkv_v[2]).astype(BF)
        total = None
        for h in range(C // HD):
            scores = dot_t(jnp.where(masks[h], q, 0.0).astype(BF), k)
            top = jnp.max(scores, axis=-1, keepdims=True)
            expo = jnp.exp(scores - top)
            denom = jnp.sum(expo, axis=-1, keepdims=True)
            mixed = dot(expo.astype(BF), v) / denom
            total = mixed if h == 0 else jnp.where(masks[h], mixed, total)
        mix[f, :, at(mp * C, C)] = total.astype(BF)
        mix_copy(f, 0).start()
        mix_copy(f, 1).start()

    fifteen = out_v.at[pl.ds(0, 240)]
    remote(fifteen, fifteen, w_s.at[2], w_r.at[2], sib).wait_recv()
    other = out_v.at[at(opp_i * C, C)]
    pass_w = remote(other, other, w_s.at[3], w_r.at[3], sib)
    pass_w.start()
    own_w.wait_recv()
    loads[2].wait()
    loads[3].wait()
    loads[4].wait()
    pass_w.wait_recv()

    def rs_copy(f):
        return remote(rs_send.at[f], rs_recv.at[f], rs_s.at[0, f], rs_r.at[0, f], sib)

    def rx_copy(f):
        return remote(rx_send.at[f], rx_recv.at[f], rs_s.at[1, f], rs_r.at[1, f], opp)

    def finish(f):
        rx_copy(f).wait_recv()
        value = own[f] + rx_recv[f].astype(F32)
        for c in range(8):
            cells[pl.ds(c, B, stride=8), :] = value[:, c * 128 : (c + 1) * 128]
        a_send[f] = cells[...].astype(BF).reshape(DP, 16, 128)
        a_recv[dp, f] = a_send[f, dp]

        @pl.loop(1, DP)
        def _(i):
            to = (dp + i) % DP
            remote(
                a_send.at[f, to], a_recv.at[dp, f], a_s.at[f], a_r.at[f], {"dp": to}
            ).start()

    @pl.loop(0, F)
    def _(f):
        mix_copy(f, 0).wait_recv()
        mix_copy(f, 2).start()
        mix_copy(f, 1).wait_recv()
        mix_copy(f, 2).wait_recv()
        for n in range(D // C):
            cols = pl.ds(n * C, C)
            res[:, cols] = dot(mix[f], out_v[:, cols]) + tok[f, :, cols].astype(F32)

        @pl.loop(0, N // 32)
        def _(i):
            rows = at(i * 32, 32)
            normed[rows] = normalize(res[rows], gain_two[...]).astype(BF)

        for n in range(D // C):
            cols = pl.ds(n * C, C)
            hidden[:, cols] = gelu(dot(normed[...], up_v[:, cols])).astype(BF)
        for n in range(D // C):
            cols = pl.ds(n * C, C)
            part[:, cols] = dot(hidden[...], down_v[:, cols])
        rs_send[f, 0] = part[at(sib_i * B, B)].astype(BF)
        rs_send[f, 1] = part[at(diag_i * B, B)].astype(BF)
        rs_copy(f).start()

        @pl.when(f > 0)
        def _():
            finish(f - 1)

        rs_copy(f).wait_recv()
        rx_send[f] = (part[at(opp_i * B, B)] + rs_recv[f, 1].astype(F32)).astype(BF)
        rx_copy(f).start()
        mine = at(mp * B, B)
        own[f] = res[mine] + part[mine] + rs_recv[f, 0].astype(F32)

    finish(F - 1)

    first.wait_send()
    own_w.wait_send()
    pass_w.wait_send()
    remote(fifteen, fifteen, w_s.at[2], w_r.at[2], sib).wait_send()
    for f in range(F):
        for kind in range(3):
            tok_copy(f, kind).wait_send()
            mix_copy(f, kind).wait_send()
        rs_copy(f).wait_send()
        rx_copy(f).wait_send()

    loads[5].wait()
    loads[6].wait()
    most = c_send.at[pl.ds(0, DP - 1)]
    count_done = remote(most, most, a_s.at[F], a_r.at[F], opp)
    count_done.wait_send()
    count_done.wait_recv()
    seen = c_recv[0]
    for i in range(1, DP):
        seen = seen + c_recv[i]
    bias = jnp.log((seen + 1.0) / (PIX + 1.0))
    block = a_send.at[0, pl.ds(0, DP - 1)]
    for f in range(F):
        done = remote(block, block, a_s.at[f], a_r.at[f], opp)
        done.wait_send()
        done.wait_recv()

    for i in range(8):
        tcells[pl.ds(i * 192, 192)] = a_recv[pl.ds(i * 4, 4)].reshape(192, 128).astype(F32)
    for p in range(2):
        for c in range(8):
            xs[pl.ds(p * S, S), pl.ds(c * 128, 128)] = tcells[
                pl.ds(p * 8 + c, S, stride=16), :
            ]

    @pl.loop(0, 2 * S // 32)
    def _(i):
        rows = at(i * 32, 32)
        n3[rows] = normalize(xs[rows], gain_three[...]).astype(BF)

    for i in range(3):
        for n in range(D // C):
            cols = pl.ds(n * C, C)
            q2[i, :, cols] = dot(n3[...], tqkv_v[i, :, cols]).astype(BF)

    one = lax.broadcasted_iota(jnp.int32, (S, S), 0) // FRAMES
    two = lax.broadcasted_iota(jnp.int32, (S, S), 1) // FRAMES
    same = one == two
    for p in range(2):
        rows = pl.ds(p * S, S)
        shift = jnp.where(same, bias[p : p + 1, :S], -1e30)
        for n in range(D // C):
            cols = pl.ds(n * C, C)
            q = q2[0, rows, cols].astype(F32) * (1.0 / math.sqrt(HD))
            k = q2[1, rows, cols]
            v = q2[2, rows, cols]
            total = None
            for h in range(C // HD):
                scores = dot_t(jnp.where(masks[h], q, 0.0).astype(BF), k) + shift
                top = jnp.max(scores, axis=-1, keepdims=True)
                expo = jnp.exp(scores - top)
                denom = jnp.sum(expo, axis=-1, keepdims=True)
                mixed = dot(expo.astype(BF), v) / denom
                total = mixed if h == 0 else jnp.where(masks[h], mixed, total)
            m2[rows, cols] = total.astype(BF)
    for n in range(D // C):
        cols = pl.ds(n * C, C)
        value = (xs[:, cols] + dot(m2[...], tout_v[:, cols])).astype(BF)
        out[:, :, cols] = value.reshape(2, S, C)


def local(
    tokens,
    clear_count,
    gain_one,
    spatial_qkv,
    spatial_out,
    gain_two,
    mlp_up,
    mlp_down,
    gain_three,
    temporal_qkv,
    temporal_out,
):
    hbm = pl.BlockSpec(memory_space=pl.ANY)
    vmem = pl.BlockSpec(memory_space=pltpu.VMEM)
    smem = pl.BlockSpec(memory_space=pltpu.SMEM)
    dma = pltpu.SemaphoreType.DMA
    scratch = [
        pltpu.VMEM((F, N, D), BF),
        pltpu.VMEM((F, N, D), BF),
        pltpu.VMEM((3, D, C), BF),
        pltpu.VMEM((D, D), BF),
        pltpu.VMEM((D, D), BF),
        pltpu.VMEM((D, D), BF),
        pltpu.VMEM((3, D, D), BF),
        pltpu.VMEM((D, D), BF),
        pltpu.VMEM((N, D), BF),
        pltpu.VMEM((N, D), BF),
        pltpu.VMEM((N, D), F32),
        pltpu.VMEM((N, D), F32),
        pltpu.VMEM((F, B, D), F32),
        pltpu.VMEM((F, 2, B, D), BF),
        pltpu.VMEM((F, 2, B, D), BF),
        pltpu.VMEM((F, B, D), BF),
        pltpu.VMEM((F, B, D), BF),
        pltpu.VMEM((B * 8, 128), F32),
        pltpu.VMEM((F, DP, 16, 128), BF),
        pltpu.VMEM((DP, F, 16, 128), BF),
        pltpu.VMEM((DP, 8, 128), F32),
        pltpu.VMEM((DP, 8, 128), F32),
        pltpu.VMEM((S * 16, 128), F32),
        pltpu.VMEM((2 * S, D), F32),
        pltpu.VMEM((2 * S, D), BF),
        pltpu.VMEM((3, 2 * S, D), BF),
        pltpu.VMEM((2 * S, D), BF),
        dma((7,)),
        dma((3, F)),
        dma((3, F)),
        dma((3, F)),
        dma((3, F)),
        dma((2, F)),
        dma((2, F)),
        dma((F + 1,)),
        dma((F + 1,)),
        dma((4,)),
        dma((4,)),
    ]
    rows = pl.pallas_call(
        kernel,
        out_shape=jax.ShapeDtypeStruct((2, S, D), BF),
        in_specs=[hbm, smem, vmem, vmem, vmem, hbm, hbm, hbm, hbm, hbm, hbm],
        out_specs=vmem,
        scratch_shapes=scratch,
        compiler_params=pltpu.CompilerParams(
            collective_id=0, has_side_effects=True, vmem_limit_bytes=60 * 1024 * 1024
        ),
        name="layers",
    )(
        tokens,
        clear_count,
        gain_one.reshape(1, D),
        gain_two.reshape(1, D),
        gain_three.reshape(1, D),
        spatial_qkv,
        spatial_out,
        mlp_up,
        mlp_down,
        temporal_qkv,
        temporal_out,
    )
    return jnp.transpose(rows, (1, 0, 2)).reshape(S, 1, 2, D)


def solution(mesh):
    placed = (
        P("dp", "mp", None),
        P("dp", "mp"),
        P(),
        P(None, None, "mp"),
        P("mp", None),
        P(),
        P(None, "mp"),
        P("mp", None),
        P(),
        P(),
        P(),
    )
    return jax.shard_map(
        local, mesh=mesh, in_specs=placed, out_specs=P(None, "mp", "dp", None), check_vma=False
    )
```

time: 205 us -> 67.3 us (0.33)
  waiting for transfers between devices: 115 us -> 0 us
  Pallas kernels: 0 us -> 63.9 us
  matrix products: 35.1 us -> 0 us
  starting transfers between devices: 14 us -> 0 us
  between operations: 13.4 us -> 0.01 us
  other arithmetic: 12 us -> 0 us
  local copies, waits for them, and re-layouts: 13.7 us -> 2.15 us
    pallas_call x0 -> x1, Pallas kernels: none -> 63.9 us  [local(): pl.pallas_call(kernel, out_shape=jax.ShapeDtypeStruct((2, S, D), BF), in_...]
    psum x1 -> x0, waiting for transfers between devices: 50.6 us -> none  [local(): lax.psum(term.astype(jnp.bfloat16), 'mp').astype(jnp.float32)]
    all_gather x1 -> x0, waiting for transfers between devices: 29 us -> none  [local(): piece = lax.all_gather(tokens, 'mp', axis=1, tiled=True)]
    dot_general x8 -> x0, matrix products: 28.1 us -> none  [the longest x1 9.68 us: local(): jnp.einsum('spf,fd->spd', hidden, mlp_down, preferred_element_type=jnp.fl...]
    reduce_scatter x1 -> x0, waiting for transfers between devices: 26.7 us -> none  [local(): lax.psum_scatter(partial_sum.astype(jnp.bfloat16), 'mp', scatter_dimensio...]
    all_to_all x2 -> x0, starting transfers between devices: 14 us -> none  [the longest x1 6.99 us: local(): lax.all_to_all(counts_local, 'dp', split_axis=1, concat_axis=0, tiled=True)]
    all_to_all x2 -> x0, waiting for transfers between devices: 8.37 us -> none  [the longest x1 8.37 us: local(): lax.all_to_all(parcel, 'dp', split_axis=1, concat_axis=0, tiled=True)]
    sub x2 -> x0, matrix products: 6.93 us -> none  [softmax_rows(): expo = jnp.exp(scores - top)]
  transfers between devices with their start and end apart: 5 -> 0, of which waited for: 4 -> 0; matrix products, arithmetic and copies ran while one was open for 2% -> 0% of each run, Pallas kernels for 0% -> 0%
where the time goes in v1:
time: 67.3 us; the launch traced here: 66.1 us
  Pallas kernels  63.9 us (95%)
  local copies, waits for them, and re-layouts  2.15 us (3%)
    pallas_call x1, Pallas kernels, local(): pl.pallas_call(kernel, out_shape=jax.ShapeDtypeStruct((2, S, D), BF), in_...  63.9 us
    reshape x1, local copies, waits for them, and re-layouts, local(): return jnp.transpose(rows, (1, 0, 2)).reshape(S, 1, 2, D)  2.15 us

profile of v1, /device:TPU:1, one launch (start us, length us, event | category | flops | bytes accessed | tf_op | source)
XLA Modules:
  0.0 66.1 jit_solution(14631236403453025520)
XLA Ops:
  0.0 63.9 %layers.1 = bf16[2,96,1024]{2,1,0:T(8,128)(2,1)} custom-call(bf16[3,64,1024]{2,1,0:T(8,128)(2,1)} %tokens.1, s32[3,64]{1,0:T(4,128)} %counts.1, f32[1,1024]{1,0:T(1,128)} %bitcast.7, f32[1,1024]{1,0:T(1,128)} %bitcast.8, f32[1,1024]{1,0:T(1,128)} %bitcast.9, bf16[3,1024,256]{2,1,0:T(8,128)(2,1)} %w_qkv.1, bf16[256,1024]{1,0:T(8,128)(2,1)} %w_out.1, ...), custom_call_target="tpu_custom_call" | custom-call | tf_op jit(solution)/shard_map/layers/pallas_call | solution.py:436
  63.9 2.1 %copy.12 = bf16[96,1,2,1024]{3,2,1,0:T(2,128)(2,1)} copy(bf16[96,1,2,1024]{3,0,2,1:T(8,128)(2,1)} %bitcast.6) | data formatting | bytes 786432 | tf_op jit(solution)/shard_map/reshape | solution.py:459

commit v2 on v1

v2 whole, which is shorter than its diff:
```python
import math

import jax
import jax.numpy as jnp
from jax import lax
from jax.experimental import pallas as pl
from jax.experimental.pallas import tpu as pltpu
from jax.sharding import PartitionSpec as P

HD = 64
PIX = 256
FRAMES = 12
EPS = 1e-06
F = 3
N = 256
H = 128
B = 64
D = 1024
C = 256
S = 96
DP = 32
BF = jnp.bfloat16
F32 = jnp.float32


def normalize(rows, gain):
    mean = jnp.sum(rows, axis=-1, keepdims=True) * (1.0 / D)
    centered = rows - mean
    spread = jnp.sum(centered * centered, axis=-1, keepdims=True) * (1.0 / D)
    return centered * lax.rsqrt(spread + EPS) * gain


def gelu(x):
    return 0.5 * x * (1.0 + lax.erf(x * (1.0 / math.sqrt(2.0))))


def at(start, size):
    return pl.ds(pl.multiple_of(start, size), size)


def dot(a, b):
    return jnp.dot(a, b, preferred_element_type=F32)


def dot_t(a, b):
    return lax.dot_general(a, b, (((1,), (1,)), ((), ())), preferred_element_type=F32)


def head_masks():
    lane = lax.broadcasted_iota(jnp.int32, (1, C), 1)
    return [(lane // HD == h) for h in range(C // HD)]


def attend(q, k, v, masks, shift):
    total = None
    for h in range(C // HD):
        scores = dot_t(jnp.where(masks[h], q, 0.0).astype(BF), k)
        if shift is not None:
            scores = scores + shift
        top = jnp.max(scores, axis=-1, keepdims=True)
        expo = jnp.exp(scores - top)
        denom = jnp.sum(expo, axis=-1, keepdims=True)
        mixed = dot(expo.astype(BF), v) * (1.0 / denom)
        total = mixed if h == 0 else jnp.where(masks[h], mixed, total)
    return total.astype(BF)


def kernel(
    tokens,
    counts,
    gain_one,
    gain_two,
    gain_three,
    w_qkv,
    w_out,
    w_up,
    w_down,
    t_qkv,
    t_out,
    out,
    tok,
    heads,
    mix,
    qkv_v,
    out_v,
    up_v,
    down_v,
    tqkv_v,
    tout_v,
    normed,
    hidden,
    res,
    part,
    own,
    rx_send,
    rx_recv,
    cells,
    a_send,
    a_recv,
    c_send,
    c_recv,
    tcells,
    xs,
    n3,
    q2,
    m2,
    loc,
    tok_s,
    tok_r,
    mix_s,
    mix_r,
    rx_s,
    rx_r,
    a_s,
    a_r,
    w_s,
    w_r,
):
    dp = lax.axis_index("dp")
    mp = lax.axis_index("mp")
    core = mp % 2
    x_hi = mp // 2
    opp_i = (mp + 2) % 4
    sib = {"mp": mp + 1 - 2 * core}
    opp = {"mp": opp_i}
    diag = {"mp": (mp + 3 - 2 * core) % 4}
    cell = (dp // 8) * 4 + dp % 4
    x_lo = (dp // 4) % 2
    half = at(core * H, H)
    other = at((1 - core) * H, H)
    own_rows = at(core * H + x_hi * B, B)
    opp_rows = at(core * H + (1 - x_hi) * B, B)
    in_half = at(x_hi * B, B)
    in_half_opp = at((1 - x_hi) * B, B)

    def remote(src, dst, ss, rs, where):
        return pltpu.make_async_remote_copy(
            src_ref=src, dst_ref=dst, send_sem=ss, recv_sem=rs, device_id=where
        )

    def local_copy(src, dst, i):
        return pltpu.make_async_copy(src, dst, loc.at[i])

    units = at(core * D, D)
    loads = [
        local_copy(tokens, tok.at[:, own_rows], 0),
        local_copy(w_qkv, qkv_v, 1),
        local_copy(w_out, out_v.at[at(mp * C, C)], 2),
        local_copy(w_up, up_v.at[core], 3),
        local_copy(w_down, down_v.at[units], 4),
        local_copy(t_qkv, tqkv_v, 5),
        local_copy(t_out, tout_v, 6),
    ]

    barrier = pltpu.get_barrier_semaphore()
    for i in range(1, 4):
        pl.semaphore_signal(barrier, inc=1, device_id={"mp": (mp + i) % 4})

    @pl.loop(1, DP)
    def _(i):
        pl.semaphore_signal(barrier, inc=1, device_id={"dp": (dp + i) % DP})

    loads[0].start()
    loads[1].start()
    pl.semaphore_wait(barrier, DP + 2)

    first = remote(
        w_out.at[at(cell * 16, 16)],
        out_v.at[at(mp * C + cell * 16, 16)],
        w_s.at[0],
        w_r.at[0],
        opp,
    )
    first.start()

    def tok_copy(f, kind):
        if kind < 2:
            return remote(
                tokens.at[f],
                tok.at[f, own_rows],
                tok_s.at[kind, f],
                tok_r.at[kind, f],
                opp if kind == 0 else sib,
            )
        blk = tok.at[f, opp_rows]
        return remote(blk, blk, tok_s.at[kind, f], tok_r.at[kind, f], sib)

    for f in range(F):
        tok_copy(f, 0).start()
    for f in range(F):
        tok_copy(f, 1).start()
    for c in loads[2:5]:
        c.start()
    to_sib = [
        remote(w_out, out_v.at[at(mp * C, C)], w_s.at[1], w_r.at[1], sib),
        remote(w_up, up_v.at[core], w_s.at[4], w_r.at[4], sib),
        remote(w_down, down_v.at[units], w_s.at[5], w_r.at[5], sib),
    ]
    for c in to_sib:
        c.start()

    row = lax.broadcasted_iota(jnp.int32, (8, 128), 0)
    lane = lax.broadcasted_iota(jnp.int32, (8, 128), 1)

    @pl.loop(0, DP)
    def _(d):
        tile = jnp.zeros((8, 128), jnp.int32)
        for f in range(F):
            for p in range(2):
                spot = (row == p) & (lane == f * DP + dp)
                tile = jnp.where(spot, counts[f, d * 2 + p], tile)
        c_send[d] = tile.astype(F32)

    c_recv[dp] = c_send[dp]

    first.wait_recv()
    mine = at(opp_i * C + cell * 16, 16)

    @pl.loop(1, 16)
    def _(j):
        q = (cell + j) % 16
        to = ((q // 4) * 2 + x_lo) * 4 + q % 4
        remote(out_v.at[mine], out_v.at[mine], w_s.at[2], w_r.at[2], {"dp": to}).start()

    @pl.loop(1, DP)
    def _(i):
        to = (dp + i) % DP
        remote(c_send.at[to], c_recv.at[dp], a_s.at[F], a_r.at[F], {"dp": to}).start()

    masks = head_masks()
    cols_mp = at(mp * C, C)

    def mix_copy(f, kind):
        src = heads.at[f, half if kind == 0 else other]
        dst = mix.at[f, :, cols_mp]
        return remote(
            src, dst, mix_s.at[kind, f], mix_r.at[kind, f], (opp, diag, sib)[kind]
        )

    loads[0].wait()
    loads[1].wait()

    @pl.loop(0, F + 1)
    def _(step):
        @pl.when(step < F)
        def _():
            tok_copy(step, 0).wait_recv()
            tok_copy(step, 2).start()

        @pl.when(step > 0)
        def _():
            f = step - 1
            tok_copy(f, 1).wait_recv()
            tok_copy(f, 2).wait_recv()
            normed[...] = normalize(tok[f].astype(F32), gain_one[...]).astype(BF)
            q = dot(normed[...], qkv_v[0]) * (1.0 / math.sqrt(HD))
            k = dot(normed[...], qkv_v[1]).astype(BF)
            v = dot(normed[...], qkv_v[2]).astype(BF)
            heads[f] = attend(q, k, v, masks, None)
            for kind in range(3):
                mix_copy(f, kind).start()
            mix[f, :, cols_mp] = heads[f, half]

    fifteen = out_v.at[pl.ds(0, 240)]
    remote(fifteen, fifteen, w_s.at[2], w_r.at[2], sib).wait_recv()
    block = out_v.at[at(opp_i * C, C)]
    pass_w = remote(block, block, w_s.at[3], w_r.at[3], sib)
    pass_w.start()
    for c in loads[5:]:
        c.start()
    for c in loads[2:5]:
        c.wait()
    for c in to_sib:
        c.wait_recv()
    pass_w.wait_recv()

    def rx_copy(f):
        return remote(rx_send.at[f], rx_recv.at[f], rx_s.at[f], rx_r.at[f], opp)

    @pl.loop(0, F)
    def _(f):
        for kind in range(3):
            mix_copy(f, kind).wait_recv()
        res[...] = dot(mix[f], out_v[...]) + tok[f, half].astype(F32)
        normed[:H] = normalize(res[...], gain_two[...]).astype(BF)
        for j in range(2):
            for n in range(D // C):
                cols = pl.ds(n * C, C)
                hidden[:, pl.ds(j * D + n * C, C)] = gelu(
                    dot(normed[:H], up_v[j, :, cols])
                ).astype(BF)
        part[...] = dot(hidden[...], down_v[...])
        rx_send[f] = part[in_half_opp].astype(BF)
        rx_copy(f).start()
        own[f] = res[in_half] + part[in_half]

    def parcels(f):
        rx_copy(f).wait_recv()
        value = own[f] + rx_recv[f].astype(F32)
        for c in range(8):
            cells[pl.ds(c, B, stride=8), :] = value[:, c * 128 : (c + 1) * 128]
        a_send[f] = cells[...].astype(BF).reshape(DP, 16, 128)
        a_recv[f, dp] = a_send[f, dp]

        @pl.loop(1, DP)
        def _(i):
            to = (dp + i) % DP
            remote(
                a_send.at[f, to], a_recv.at[f, dp], a_s.at[f], a_r.at[f], {"dp": to}
            ).start()

    for f in range(F):
        parcels(f)

    first.wait_send()
    for c in to_sib:
        c.wait_send()
    pass_w.wait_send()
    remote(fifteen, fifteen, w_s.at[2], w_r.at[2], sib).wait_send()
    for f in range(F):
        for kind in range(3):
            tok_copy(f, kind).wait_send()
            mix_copy(f, kind).wait_send()
        rx_copy(f).wait_send()

    loads[5].wait()
    loads[6].wait()
    most = c_send.at[pl.ds(0, DP - 1)]
    count_done = remote(most, most, a_s.at[F], a_r.at[F], opp)
    count_done.wait_send()
    count_done.wait_recv()
    seen = c_recv[0]
    for i in range(1, DP):
        seen = seen + c_recv[i]
    bias = jnp.log((seen + 1.0) / (PIX + 1.0))
    group = lax.broadcasted_iota(jnp.int32, (S, S), 0) % DP // (FRAMES // F)
    key_group = lax.broadcasted_iota(jnp.int32, (S, S), 1) % DP // (FRAMES // F)
    same = group == key_group

    def arrive(f):
        block = a_send.at[f, pl.ds(0, DP - 1)]
        done = remote(block, block, a_s.at[f], a_r.at[f], opp)
        done.wait_send()
        done.wait_recv()
        tcells[...] = a_recv[f].reshape(DP * 16, 128).astype(F32)
        for p in range(2):
            for c in range(8):
                xs[pl.ds(p * S + f * DP, DP), pl.ds(c * 128, 128)] = tcells[
                    pl.ds(p * 8 + c, DP, stride=16), :
                ]
            n3[pl.ds(f * 2 * DP + p * DP, DP)] = normalize(
                xs[pl.ds(p * S + f * DP, DP)], gain_three[...]
            ).astype(BF)

    def project(frames):
        rows = n3[pl.ds(frames[0] * 2 * DP, len(frames) * 2 * DP)]
        for i in range(3):
            for n in range(D // C):
                cols = pl.ds(n * C, C)
                value = dot(rows, tqkv_v[i, :, cols])
                if i == 0:
                    value = value * (1.0 / math.sqrt(HD))
                value = value.astype(BF)
                for j, f in enumerate(frames):
                    for p in range(2):
                        start = (j * 2 + p) * DP
                        q2[i, pl.ds(p * S + f * DP, DP), cols] = value[start : start + DP]

    arrive(0)
    arrive(1)
    project((0, 1))
    arrive(2)
    project((2,))

    for p in range(2):
        rows = pl.ds(p * S, S)
        shift = jnp.where(same, bias[p : p + 1, :S], -1e30)
        for n in range(D // C):
            cols = pl.ds(n * C, C)
            q = q2[0, rows, cols].astype(F32)
            m2[rows, cols] = attend(q, q2[1, rows, cols], q2[2, rows, cols], masks, shift)
    value = (xs[...] + dot(m2[...], tout_v[...])).astype(BF)
    out[...] = value.reshape(2, S, D)


def local(
    tokens,
    clear_count,
    gain_one,
    spatial_qkv,
    spatial_out,
    gain_two,
    mlp_up,
    mlp_down,
    gain_three,
    temporal_qkv,
    temporal_out,
):
    hbm = pl.BlockSpec(memory_space=pl.ANY)
    vmem = pl.BlockSpec(memory_space=pltpu.VMEM)
    smem = pl.BlockSpec(memory_space=pltpu.SMEM)
    dma = pltpu.SemaphoreType.DMA
    scratch = [
        pltpu.VMEM((F, N, D), BF),
        pltpu.VMEM((F, N, C), BF),
        pltpu.VMEM((F, H, D), BF),
        pltpu.VMEM((3, D, C), BF),
        pltpu.VMEM((D, D), BF),
        pltpu.VMEM((2, D, D), BF),
        pltpu.VMEM((2 * D, D), BF),
        pltpu.VMEM((3, D, D), BF),
        pltpu.VMEM((D, D), BF),
        pltpu.VMEM((N, D), BF),
        pltpu.VMEM((H, 2 * D), BF),
        pltpu.VMEM((H, D), F32),
        pltpu.VMEM((H, D), F32),
        pltpu.VMEM((F, B, D), F32),
        pltpu.VMEM((F, B, D), BF),
        pltpu.VMEM((F, B, D), BF),
        pltpu.VMEM((B * 8, 128), F32),
        pltpu.VMEM((F, DP, 16, 128), BF),
        pltpu.VMEM((F, DP, 16, 128), BF),
        pltpu.VMEM((DP, 8, 128), F32),
        pltpu.VMEM((DP, 8, 128), F32),
        pltpu.VMEM((DP * 16, 128), F32),
        pltpu.VMEM((2 * S, D), F32),
        pltpu.VMEM((2 * S, D), BF),
        pltpu.VMEM((3, 2 * S, D), BF),
        pltpu.VMEM((2 * S, D), BF),
        dma((7,)),
        dma((3, F)),
        dma((3, F)),
        dma((3, F)),
        dma((3, F)),
        dma((F,)),
        dma((F,)),
        dma((F + 1,)),
        dma((F + 1,)),
        dma((6,)),
        dma((6,)),
    ]
    rows = pl.pallas_call(
        kernel,
        out_shape=jax.ShapeDtypeStruct((2, S, D), BF),
        in_specs=[hbm, smem, vmem, vmem, vmem, hbm, hbm, hbm, hbm, hbm, hbm],
        out_specs=vmem,
        scratch_shapes=scratch,
        compiler_params=pltpu.CompilerParams(
            collective_id=0, has_side_effects=True, vmem_limit_bytes=60 * 1024 * 1024
        ),
        name="layers",
    )(
        tokens,
        clear_count,
        gain_one.reshape(1, D),
        gain_two.reshape(1, D),
        gain_three.reshape(1, D),
        spatial_qkv,
        spatial_out,
        mlp_up,
        mlp_down,
        temporal_qkv,
        temporal_out,
    )
    rows = rows.reshape(2, F, DP, D)
    return jnp.transpose(rows, (2, 1, 0, 3)).reshape(S, 1, 2, D)


def solution(mesh):
    placed = (
        P("dp", "mp", None),
        P("dp", "mp"),
        P(),
        P(None, None, "mp"),
        P("mp", None),
        P(),
        P(None, "mp"),
        P("mp", None),
        P(),
        P(),
        P(),
    )
    return jax.shard_map(
        local, mesh=mesh, in_specs=placed, out_specs=P(None, "mp", "dp", None), check_vma=False
    )
```

time: 67.3 us -> 52 us (0.77); the launches traced: 66.1 us -> 51.8 us
  Pallas kernels: 63.9 us -> 49.6 us
    pallas_call x1, Pallas kernels: 63.9 us -> 49.6 us  [local(): pl.pallas_call(kernel, out_shape=jax.ShapeDtypeStruct((2, S, D), BF), in_...]
    reshape x1 -> x0, local copies, waits for them, and re-layouts: 2.15 us -> none  [local(): return jnp.transpose(rows, (1, 0, 2)).reshape(S, 1, 2, D)]
    transpose x0 -> x1, local copies, waits for them, and re-layouts: none -> 2.15 us  [local(): return jnp.transpose(rows, (2, 1, 0, 3)).reshape(S, 1, 2, D)]
where the time goes in v2:
time: 52 us; the launch traced here: 51.8 us
  Pallas kernels  49.6 us (95%)
  local copies, waits for them, and re-layouts  2.15 us (4%)
    pallas_call x1, Pallas kernels, local(): pl.pallas_call(kernel, out_shape=jax.ShapeDtypeStruct((2, S, D), BF), in_...  49.6 us
    transpose x1, local copies, waits for them, and re-layouts, local(): return jnp.transpose(rows, (2, 1, 0, 3)).reshape(S, 1, 2, D)  2.15 us

profile of v2, /device:TPU:1, one launch (start us, length us, event | category | flops | bytes accessed | tf_op | source)
XLA Modules:
  0.0 51.8 jit_solution(8401030450324981218)
XLA Ops:
  0.0 49.6 %layers.1 = bf16[2,96,1024]{2,1,0:T(8,128)(2,1)} custom-call(bf16[3,64,1024]{2,1,0:T(8,128)(2,1)} %tokens.1, s32[3,64]{1,0:T(4,128)} %counts.1, f32[1,1024]{1,0:T(1,128)} %bitcast.8, f32[1,1024]{1,0:T(1,128)} %bitcast.9, f32[1,1024]{1,0:T(1,128)} %bitcast.10, bf16[3,1024,256]{2,1,0:T(8,128)(2,1)} %w_qkv.1, bf16[256,1024]{1,0:T(8,128)(2,1)} %w_out.1, ...), custom_call_target="tpu_custom_call" | custom-call | tf_op jit(solution)/shard_map/layers/pallas_call | solution.py:442
  49.7 2.1 %copy.12 = bf16[32,3,2,1024]{3,2,1,0:T(2,128)(2,1)} copy(bf16[32,3,2,1024]{3,0,1,2:T(8,128)(2,1)} %bitcast.7) | data formatting | bytes 786432 | tf_op jit(solution)/shard_map/transpose | solution.py:466

commit v3 on v2

--- a/solution.py
+++ b/solution.py
@@ -115,6 +115,7 @@
     a_r,
     w_s,
     w_r,
+    rounds,
 ):
     dp = lax.axis_index("dp")
     mp = lax.axis_index("mp")
@@ -156,13 +157,15 @@
     for i in range(1, 4):
         pl.semaphore_signal(barrier, inc=1, device_id={"mp": (mp + i) % 4})
 
-    @pl.loop(1, DP)
-    def _(i):
-        pl.semaphore_signal(barrier, inc=1, device_id={"dp": (dp + i) % DP})
-
+    y, z = dp // 8, dp % 4
+    near = [{"dp": (((y + i) % 4) * 2 + x_lo) * 4 + z} for i in (1, 2, 3)]
+    near += [{"dp": dp - z + (z + i) % 4} for i in (1, 2, 3)]
+    near += [{"dp": (y * 2 + 1 - x_lo) * 4 + z}]
+    for who in near:
+        pl.semaphore_signal(barrier, inc=1, device_id=who)
     loads[0].start()
     loads[1].start()
-    pl.semaphore_wait(barrier, DP + 2)
+    pl.semaphore_wait(barrier, 3 + len(near))
 
     first = remote(
         w_out.at[at(cell * 16, 16)],
@@ -189,6 +192,8 @@
         tok_copy(f, 0).start()
     for f in range(F):
         tok_copy(f, 1).start()
+    for who in near:
+        pl.semaphore_signal(rounds.at[0], inc=1, device_id=who)
     for c in loads[2:5]:
         c.start()
     to_sib = [
@@ -213,6 +218,9 @@
 
     c_recv[dp] = c_send[dp]
 
+    pl.semaphore_wait(rounds.at[0], len(near))
+    for who in near:
+        pl.semaphore_signal(rounds.at[1], inc=1, device_id=who)
     first.wait_recv()
     mine = at(opp_i * C + cell * 16, 16)
 
@@ -221,6 +229,8 @@
         q = (cell + j) % 16
         to = ((q // 4) * 2 + x_lo) * 4 + q % 4
         remote(out_v.at[mine], out_v.at[mine], w_s.at[2], w_r.at[2], {"dp": to}).start()
+
+    pl.semaphore_wait(rounds.at[1], len(near))
 
     @pl.loop(1, DP)
     def _(i):
@@ -367,10 +377,10 @@
                         q2[i, pl.ds(p * S + f * DP, DP), cols] = value[start : start + DP]
 
     arrive(0)
+    project((0,))
     arrive(1)
-    project((0, 1))
     arrive(2)
-    project((2,))
+    project((1, 2))
 
     for p in range(2):
         rows = pl.ds(p * S, S)
@@ -438,6 +448,7 @@
         dma((F + 1,)),
         dma((6,)),
         dma((6,)),
+        pltpu.SemaphoreType.REGULAR((2,)),
     ]
     rows = pl.pallas_call(
         kernel,

time: 52 us -> 50.9 us (0.979)
  Pallas kernels: 49.6 us -> 48.5 us
    pallas_call x1, Pallas kernels: 49.6 us -> 48.5 us  [local(): pl.pallas_call(kernel, out_shape=jax.ShapeDtypeStruct((2, S, D), BF), in_...]
where the time goes in v3:
time: 50.9 us; the launch traced here: 50.7 us
  Pallas kernels  48.5 us (95%)
  local copies, waits for them, and re-layouts  2.15 us (4%)
    pallas_call x1, Pallas kernels, local(): pl.pallas_call(kernel, out_shape=jax.ShapeDtypeStruct((2, S, D), BF), in_...  48.5 us
    transpose x1, local copies, waits for them, and re-layouts, local(): return jnp.transpose(rows, (2, 1, 0, 3)).reshape(S, 1, 2, D)  2.15 us

profile of v3, /device:TPU:1, one launch (start us, length us, event | category | flops | bytes accessed | tf_op | source)
XLA Modules:
  0.0 50.7 jit_solution(10081000181319806535)
XLA Ops:
  0.0 48.5 %layers.1 = bf16[2,96,1024]{2,1,0:T(8,128)(2,1)} custom-call(bf16[3,64,1024]{2,1,0:T(8,128)(2,1)} %tokens.1, s32[3,64]{1,0:T(4,128)} %counts.1, f32[1,1024]{1,0:T(1,128)} %bitcast.8, f32[1,1024]{1,0:T(1,128)} %bitcast.9, f32[1,1024]{1,0:T(1,128)} %bitcast.10, bf16[3,1024,256]{2,1,0:T(8,128)(2,1)} %w_qkv.1, bf16[256,1024]{1,0:T(8,128)(2,1)} %w_out.1, ...), custom_call_target="tpu_custom_call" | custom-call | tf_op jit(solution)/shard_map/layers/pallas_call | solution.py:453
  48.6 2.1 %copy.12 = bf16[32,3,2,1024]{3,2,1,0:T(2,128)(2,1)} copy(bf16[32,3,2,1024]{3,0,1,2:T(8,128)(2,1)} %bitcast.7) | data formatting | bytes 786432 | tf_op jit(solution)/shard_map/transpose | solution.py:477

commit v4 on v3

--- a/solution.py
+++ b/solution.py
@@ -88,6 +88,7 @@
     tqkv_v,
     tout_v,
     normed,
+    q1,
     hidden,
     res,
     part,
@@ -131,6 +132,8 @@
     other = at((1 - core) * H, H)
     own_rows = at(core * H + x_hi * B, B)
     opp_rows = at(core * H + (1 - x_hi) * B, B)
+    sib_rows = at((1 - core) * H + x_hi * B, B)
+    diag_rows = at((1 - core) * H + (1 - x_hi) * B, B)
     in_half = at(x_hi * B, B)
     in_half_opp = at((1 - x_hi) * B, B)
 
@@ -247,29 +250,35 @@
             src, dst, mix_s.at[kind, f], mix_r.at[kind, f], (opp, diag, sib)[kind]
         )
 
+    def spatial_project(f, blocks):
+        parts = [normalize(tok[f, b].astype(F32), gain_one[...]).astype(BF) for b in blocks]
+        rows = jnp.concatenate(parts, axis=0)
+        for i in range(3):
+            value = dot(rows, qkv_v[i])
+            if i == 0:
+                value = value * (1.0 / math.sqrt(HD))
+            value = value.astype(BF)
+            for j, b in enumerate(blocks):
+                q1[i, f, b] = value[j * B : (j + 1) * B]
+
     loads[0].wait()
     loads[1].wait()
 
-    @pl.loop(0, F + 1)
-    def _(step):
-        @pl.when(step < F)
-        def _():
-            tok_copy(step, 0).wait_recv()
-            tok_copy(step, 2).start()
-
-        @pl.when(step > 0)
-        def _():
-            f = step - 1
-            tok_copy(f, 1).wait_recv()
-            tok_copy(f, 2).wait_recv()
-            normed[...] = normalize(tok[f].astype(F32), gain_one[...]).astype(BF)
-            q = dot(normed[...], qkv_v[0]) * (1.0 / math.sqrt(HD))
-            k = dot(normed[...], qkv_v[1]).astype(BF)
-            v = dot(normed[...], qkv_v[2]).astype(BF)
-            heads[f] = attend(q, k, v, masks, None)
-            for kind in range(3):
-                mix_copy(f, kind).start()
-            mix[f, :, cols_mp] = heads[f, half]
+    @pl.loop(0, F)
+    def _(f):
+        tok_copy(f, 1).wait_recv()
+        spatial_project(f, (own_rows, sib_rows))
+
+    @pl.loop(0, F)
+    def _(f):
+        tok_copy(f, 0).wait_recv()
+        tok_copy(f, 2).start()
+        tok_copy(f, 2).wait_recv()
+        spatial_project(f, (opp_rows, diag_rows))
+        heads[f] = attend(q1[0, f].astype(F32), q1[1, f], q1[2, f], masks, None)
+        for kind in range(3):
+            mix_copy(f, kind).start()
+        mix[f, :, cols_mp] = heads[f, half]
 
     fifteen = out_v.at[pl.ds(0, 240)]
     remote(fifteen, fifteen, w_s.at[2], w_r.at[2], sib).wait_recv()
@@ -292,12 +301,12 @@
         for kind in range(3):
             mix_copy(f, kind).wait_recv()
         res[...] = dot(mix[f], out_v[...]) + tok[f, half].astype(F32)
-        normed[:H] = normalize(res[...], gain_two[...]).astype(BF)
+        normed[...] = normalize(res[...], gain_two[...]).astype(BF)
         for j in range(2):
             for n in range(D // C):
                 cols = pl.ds(n * C, C)
                 hidden[:, pl.ds(j * D + n * C, C)] = gelu(
-                    dot(normed[:H], up_v[j, :, cols])
+                    dot(normed[...], up_v[j, :, cols])
                 ).astype(BF)
         part[...] = dot(hidden[...], down_v[...])
         rx_send[f] = part[in_half_opp].astype(BF)
@@ -420,7 +429,8 @@
         pltpu.VMEM((2 * D, D), BF),
         pltpu.VMEM((3, D, D), BF),
         pltpu.VMEM((D, D), BF),
-        pltpu.VMEM((N, D), BF),
+        pltpu.VMEM((H, D), BF),
+        pltpu.VMEM((3, F, N, C), BF),
         pltpu.VMEM((H, 2 * D), BF),
         pltpu.VMEM((H, D), F32),
         pltpu.VMEM((H, D), F32),

time: 50.9 us -> 49.4 us (0.971)
  Pallas kernels: 48.5 us -> 46.9 us
    pallas_call x1, Pallas kernels: 48.5 us -> 46.9 us  [local(): pl.pallas_call(kernel, out_shape=jax.ShapeDtypeStruct((2, S, D), BF), in_...]
where the time goes in v4:
time: 49.4 us; the launch traced here: 49.1 us
  Pallas kernels  46.9 us (95%)
  local copies, waits for them, and re-layouts  2.15 us (4%)
    pallas_call x1, Pallas kernels, local(): pl.pallas_call(kernel, out_shape=jax.ShapeDtypeStruct((2, S, D), BF), in_...  46.9 us
    transpose x1, local copies, waits for them, and re-layouts, local(): return jnp.transpose(rows, (2, 1, 0, 3)).reshape(S, 1, 2, D)  2.15 us

profile of v4, /device:TPU:1, one launch (start us, length us, event | category | flops | bytes accessed | tf_op | source)
XLA Modules:
  0.0 49.1 jit_solution(763794844224945170)
XLA Ops:
  0.0 46.9 %layers.1 = bf16[2,96,1024]{2,1,0:T(8,128)(2,1)} custom-call(bf16[3,64,1024]{2,1,0:T(8,128)(2,1)} %tokens.1, s32[3,64]{1,0:T(4,128)} %counts.1, f32[1,1024]{1,0:T(1,128)} %bitcast.8, f32[1,1024]{1,0:T(1,128)} %bitcast.9, f32[1,1024]{1,0:T(1,128)} %bitcast.10, bf16[3,1024,256]{2,1,0:T(8,128)(2,1)} %w_qkv.1, bf16[256,1024]{1,0:T(8,128)(2,1)} %w_out.1, ...), custom_call_target="tpu_custom_call" | custom-call | tf_op jit(solution)/shard_map/layers/pallas_call | solution.py:463
  46.9 2.1 %copy.12 = bf16[32,3,2,1024]{3,2,1,0:T(2,128)(2,1)} copy(bf16[32,3,2,1024]{3,0,1,2:T(8,128)(2,1)} %bitcast.7) | data formatting | bytes 786432 | tf_op jit(solution)/shard_map/transpose | solution.py:487

commit v5 on v4

--- a/solution.py
+++ b/solution.py
@@ -207,12 +207,12 @@
     for c in to_sib:
         c.start()
 
-    row = lax.broadcasted_iota(jnp.int32, (8, 128), 0)
-    lane = lax.broadcasted_iota(jnp.int32, (8, 128), 1)
+    row = lax.broadcasted_iota(jnp.int32, (2, 128), 0)
+    lane = lax.broadcasted_iota(jnp.int32, (2, 128), 1)
 
     @pl.loop(0, DP)
     def _(d):
-        tile = jnp.zeros((8, 128), jnp.int32)
+        tile = jnp.zeros((2, 128), jnp.int32)
         for f in range(F):
             for p in range(2):
                 spot = (row == p) & (lane == f * DP + dp)
@@ -440,8 +440,8 @@
         pltpu.VMEM((B * 8, 128), F32),
         pltpu.VMEM((F, DP, 16, 128), BF),
         pltpu.VMEM((F, DP, 16, 128), BF),
-        pltpu.VMEM((DP, 8, 128), F32),
-        pltpu.VMEM((DP, 8, 128), F32),
+        pltpu.VMEM((DP, 2, 128), F32),
+        pltpu.VMEM((DP, 2, 128), F32),
         pltpu.VMEM((DP * 16, 128), F32),
         pltpu.VMEM((2 * S, D), F32),
         pltpu.VMEM((2 * S, D), BF),

time: 49.4 us -> 49.2 us (level)
  Pallas kernels: 46.9 us -> 46.3 us
    pallas_call x1, Pallas kernels: 46.9 us -> 46.3 us  [local(): pl.pallas_call(kernel, out_shape=jax.ShapeDtypeStruct((2, S, D), BF), in_...]
where the time goes in v5:
time: 49.2 us; the launch traced here: 48.4 us
  Pallas kernels  46.3 us (94%)
  local copies, waits for them, and re-layouts  2.15 us (4%)
    pallas_call x1, Pallas kernels, local(): pl.pallas_call(kernel, out_shape=jax.ShapeDtypeStruct((2, S, D), BF), in_...  46.3 us
    transpose x1, local copies, waits for them, and re-layouts, local(): return jnp.transpose(rows, (2, 1, 0, 3)).reshape(S, 1, 2, D)  2.15 us

profile of v5, /device:TPU:1, one launch (start us, length us, event | category | flops | bytes accessed | tf_op | source)
XLA Modules:
  0.0 48.4 jit_solution(744509375011887556)
XLA Ops:
  0.0 46.3 %layers.1 = bf16[2,96,1024]{2,1,0:T(8,128)(2,1)} custom-call(bf16[3,64,1024]{2,1,0:T(8,128)(2,1)} %tokens.1, s32[3,64]{1,0:T(4,128)} %counts.1, f32[1,1024]{1,0:T(1,128)} %bitcast.8, f32[1,1024]{1,0:T(1,128)} %bitcast.9, f32[1,1024]{1,0:T(1,128)} %bitcast.10, bf16[3,1024,256]{2,1,0:T(8,128)(2,1)} %w_qkv.1, bf16[256,1024]{1,0:T(8,128)(2,1)} %w_out.1, ...), custom_call_target="tpu_custom_call" | custom-call | tf_op jit(solution)/shard_map/layers/pallas_call | solution.py:463
  46.3 2.1 %copy.12 = bf16[32,3,2,1024]{3,2,1,0:T(2,128)(2,1)} copy(bf16[32,3,2,1024]{3,0,1,2:T(8,128)(2,1)} %bitcast.7) | data formatting | bytes 786432 | tf_op jit(solution)/shard_map/transpose | solution.py:487

commit v6 on v5

--- a/solution.py
+++ b/solution.py
@@ -90,6 +90,7 @@
     normed,
     q1,
     hidden,
+    pre,
     res,
     part,
     own,
@@ -291,6 +292,11 @@
         c.wait()
     for c in to_sib:
         c.wait_recv()
+    chip = at(x_hi * 2 * C, 2 * C)
+    away = at((1 - x_hi) * 2 * C, 2 * C)
+    for f in range(F):
+        mix_copy(f, 2).wait_recv()
+        pre[f] = dot(mix[f, :, chip], out_v[chip]) + tok[f, half].astype(F32)
     pass_w.wait_recv()
 
     def rx_copy(f):
@@ -298,9 +304,9 @@
 
     @pl.loop(0, F)
     def _(f):
-        for kind in range(3):
+        for kind in range(2):
             mix_copy(f, kind).wait_recv()
-        res[...] = dot(mix[f], out_v[...]) + tok[f, half].astype(F32)
+        res[...] = pre[f] + dot(mix[f, :, away], out_v[away])
         normed[...] = normalize(res[...], gain_two[...]).astype(BF)
         for j in range(2):
             for n in range(D // C):
@@ -432,6 +438,7 @@
         pltpu.VMEM((H, D), BF),
         pltpu.VMEM((3, F, N, C), BF),
         pltpu.VMEM((H, 2 * D), BF),
+        pltpu.VMEM((F, H, D), F32),
         pltpu.VMEM((H, D), F32),
         pltpu.VMEM((H, D), F32),
         pltpu.VMEM((F, B, D), F32),

time: 49.2 us -> 49.1 us (level)
  no operation moved by 1% of the time
where the time goes in v6:
time: 49.1 us; the launch traced here: 48.3 us
  Pallas kernels  46.1 us (94%)
  local copies, waits for them, and re-layouts  2.15 us (4%)
    pallas_call x1, Pallas kernels, local(): pl.pallas_call(kernel, out_shape=jax.ShapeDtypeStruct((2, S, D), BF), in_...  46.1 us
    transpose x1, local copies, waits for them, and re-layouts, local(): return jnp.transpose(rows, (2, 1, 0, 3)).reshape(S, 1, 2, D)  2.15 us

profile of v6, /device:TPU:1, one launch (start us, length us, event | category | flops | bytes accessed | tf_op | source)
XLA Modules:
  0.0 48.3 jit_solution(16149540891230121465)
XLA Ops:
  0.0 46.1 %layers.1 = bf16[2,96,1024]{2,1,0:T(8,128)(2,1)} custom-call(bf16[3,64,1024]{2,1,0:T(8,128)(2,1)} %tokens.1, s32[3,64]{1,0:T(4,128)} %counts.1, f32[1,1024]{1,0:T(1,128)} %bitcast.8, f32[1,1024]{1,0:T(1,128)} %bitcast.9, f32[1,1024]{1,0:T(1,128)} %bitcast.10, bf16[3,1024,256]{2,1,0:T(8,128)(2,1)} %w_qkv.1, bf16[256,1024]{1,0:T(8,128)(2,1)} %w_out.1, ...), custom_call_target="tpu_custom_call" | custom-call | tf_op jit(solution)/shard_map/layers/pallas_call | solution.py:470
  46.1 2.1 %copy.12 = bf16[32,3,2,1024]{3,2,1,0:T(2,128)(2,1)} copy(bf16[32,3,2,1024]{3,0,1,2:T(8,128)(2,1)} %bitcast.7) | data formatting | bytes 786432 | tf_op jit(solution)/shard_map/transpose | solution.py:494
